TPU v7x, 512 devices: a whole 4x8x8 slice. The times are simulated.
512 devices in a mesh: sweep: 8 (over z_lo, core), recv: 64 (over x, y, z_hi).
Axes of the slice: x: 4, y: 8, z: 8 (z_hi: 2, z_lo: 4; z = z_hi * 4 + z_lo), core: 2. Of those that a mesh axis runs over, the one named last changes fastest.
Arguments:
- records: bfloat16 [16, 4096, 4096], P('sweep', 'recv'), may hold values from -6 to 6
- pilots: bfloat16 [16, 3968], replicated, may hold values from -0.09375 to 0.09375
- hadamard: int32 [16, 16], replicated, may hold values from -1 to 1, as said below
- code_vibrator: int32 [16], replicated, may hold values from 0 to 15, each once
- owner_map: int32 [4096], P('recv'), may hold values from 0 to 15
- live_mask: int32 [4096], P('recv'), may hold values 0 or 1
- filters: bfloat16 [16, 128, 128], P('sweep'), may hold values from -0.5 to 0.5
- targets: bfloat16 [16, 4096, 128], P('sweep', 'recv'), may hold values from -6 to 6
Outputs:
- responses: float32 [16, 4096, 128], P('sweep', 'recv')
- gradient: float32 [16, 128, 128], P('sweep', 'recv')
Inputs may be any that keep to these rules, and one draw needn't show every extreme that they name: hadamard transposed times hadamard is 16 times the identity. `code_vibrator`: every vibrator belongs to exactly one code.
All inputs are finite; a program needn't handle non-finite values. No bound on the sum of `live_mask` on one device may be relied on, other than what follows from the above.
Results may differ from a plain program's by a relative error of at most 0.0085.
Values may be sent and summed in bfloat16 or wider, within the bound.
A program may use at most 64 MiB of HBM per device.

v0:
```python
import math

import jax
import jax.numpy as jnp
from jax import lax
from jax.sharding import PartitionSpec as P


def toeplitz(sweep_pilot, samples, lagcount):
    padding = jnp.zeros((samples + 1 - sweep_pilot.shape[0],), sweep_pilot.dtype)
    extended = jnp.concatenate([sweep_pilot, padding])
    return jnp.tile(extended, lagcount)[: lagcount * samples].reshape(lagcount, samples)


def correlate_split(combined, sweep_pilot, samples, lagcount):
    upper = combined.astype(jnp.bfloat16)
    lower = (combined - upper.astype(jnp.float32)).astype(jnp.bfloat16)
    paired = jnp.concatenate([upper, lower], axis=0)
    toe_rows = toeplitz(sweep_pilot, samples, lagcount)
    lagged = lax.dot_general(
        paired, toe_rows, (((1,), (1,)), ((), ())), preferred_element_type=jnp.float32
    )
    half = combined.shape[0]
    return lagged[:half] + lagged[half:]


def local(records, pilots, hadamard, code_vibrator, owner_map, live_mask, filters, targets):
    codes = hadamard.shape[1]
    held_sweeps = records.shape[0]
    channels = records.shape[1]
    samples = records.shape[2]
    lagcount = filters.shape[1]
    owned_codes = filters.shape[0]
    first_code = lax.axis_index("sweep") * owned_codes
    code_norm = 1.0 / math.sqrt(codes)
    onehot = (code_vibrator[:, None] == jnp.arange(codes, dtype=jnp.int32)[None, :]).astype(
        jnp.bfloat16
    )
    code_pilot = jnp.dot(onehot, pilots, preferred_element_type=jnp.float32).astype(jnp.bfloat16)
    sign_table = hadamard.astype(jnp.bfloat16)
    sign_rows = lax.dynamic_slice_in_dim(
        sign_table, lax.axis_index("sweep") * held_sweeps, held_sweeps, 0
    )

    def column(operands):
        sweep_pilot, signs_col = operands
        combined = jnp.einsum("s,srt->rt", signs_col, records, preferred_element_type=jnp.float32)
        return code_norm * correlate_split(combined, sweep_pilot, samples, lagcount)

    decoded = lax.psum_scatter(
        lax.map(column, (code_pilot, sign_rows.T)), "sweep", scatter_dimension=0, tiled=True
    ).astype(jnp.bfloat16)
    col_vibs = lax.dynamic_slice_in_dim(code_vibrator, first_code, owned_codes, 0)
    responses = jnp.einsum("crl,clm->crm", decoded, filters, preferred_element_type=jnp.float32)
    owned = (owner_map[None, :] == col_vibs[:, None]).astype(jnp.float32)
    weight = live_mask.astype(jnp.float32)[None, :] * (0.25 + owned)
    residual = (weight[:, :, None] * (responses - targets.astype(jnp.float32))).astype(jnp.bfloat16)
    factor = 1.0 / math.sqrt(channels * lax.axis_size("recv"))
    local_grad = (
        jnp.einsum("crl,crm->clm", decoded, residual, preferred_element_type=jnp.float32) * factor
    )
    summed = lax.psum(local_grad, "recv")
    share_rows = lagcount // lax.axis_size("recv")
    gradient = lax.dynamic_slice_in_dim(summed, lax.axis_index("recv") * share_rows, share_rows, 1)
    return (responses, gradient)


def solution(mesh):
    in_specs = (
        P("sweep", "recv", None),
        P(),
        P(),
        P(),
        P("recv"),
        P("recv"),
        P("sweep", None, None),
        P("sweep", "recv", None),
    )
    out_specs = (P("sweep", "recv", None), P("sweep", "recv", None))
    return jax.shard_map(local, mesh=mesh, in_specs=in_specs, out_specs=out_specs, check_vma=False)
```

profile of v0, /device:TPU:8, one launch (start us, length us, event | category | flops | bytes accessed | tf_op | source)
XLA Modules:
  0.0 939.9 jit_solution(15561842590453519801)
XLA Ops:
  9.0 97.8 %while.10 = (s32[]{:T(128)}, f32[16,64,128]{2,1,0:T(8,128)}, bf16[16,2]{1,0:T(8,128)(2,1)S(1)}, bf16[2,64,4096]{2,1,0:T(8,128)(2,1)}, bf16[16,3968]{1,0:T(8,128)(2,1)S(1)}, /*index=5*/s32[]{:T(128)}, bf16[]{:T(256)}) while((s32[]{:T(128)}, f32[16,64,128]{2,1,0:T(8,128)}, bf16[16,2]{1,0:T(8,128)(2,1)S(1)}, bf16[2,64,4096]{2,1,0:T(8,128)(2,1)}, ...), condition=%wide.region_1.2_spmd, body=%wide.region_0.1_spmd.sunk | while | flops 138428416 | bytes 19079812 | solution.py:51
  9.2 1.1 tile.12
  11.6 1.3 fusion.35
  15.3 1.1 tile.12
  17.8 1.3 fusion.35
  21.4 1.1 tile.12
  23.9 1.3 fusion.35
  27.5 1.1 tile.12
  30.0 1.3 fusion.35
  33.6 1.1 tile.12
  36.1 1.3 fusion.35
  39.8 1.1 tile.12
  42.2 1.3 fusion.35
  45.9 1.1 tile.12
  48.3 1.3 fusion.35
  52.0 1.1 tile.12
  54.4 1.3 fusion.35
  58.1 1.1 tile.12
  60.6 1.3 fusion.35
  64.2 1.1 tile.12
  66.7 1.3 fusion.35
  70.3 1.1 tile.12
  72.8 1.3 fusion.35
  78.9 1.3 fusion.35
  85.0 1.3 fusion.35
  91.1 1.3 fusion.35
  97.2 1.3 fusion.35
  103.4 1.3 fusion.35
  107.1 43.9 %reduce-scatter.2.cloned.1.call-done = f32[2,64,128]{2,1,0:T(8,128)} async-done(((f32[16,64,128]{2,1,0:T(8,128)}), f32[2,64,128]{2,1,0:T(8,128)}) %reduce-scatter.2.cloned.1.call-update) | async-done | bytes 65552 | tf_op jit(solution)/shard_map/reduce_scatter | solution.py:50
  152.0 1.8 convolution_multiply_fusion
  153.8 778.0 %all-reduce.3.cloned.1.call-done = f32[2,128,128]{2,1,0:T(8,128)} async-done(((f32[2,128,128]{2,1,0:T(8,128)}), f32[2,128,128]{2,1,0:T(8,128)}) %all-reduce.3.cloned.1.call-update) | async-done | bytes 131088 | tf_op jit(solution)/shard_map/psum | solution.py:62
  931.8 1.3 constant_dynamic-slice_fusion.1
  (208 shorter events, 67.0 us)
Async XLA Ops:
  7.2 0.9 copy-start
  7.2 143.8 %reduce-scatter.2.cloned.1.call-start = ((), (), s32[]{:S(2)}) async-start(), calls=%async_computation.1 | async-start | bytes 589824 | tf_op jit(solution)/shard_map/reduce_scatter | solution.py:50
  9.0 98.0 %copy-start.4 = (s32[16]{0:T(128)S(1)}, s32[16]{0:T(128)}, u32[]{:S(2)}) copy-start(s32[16]{0:T(128)} %param.13) | copy-start | bytes 196
  9.0 98.1 %copy-start.7 = (s32[64]{0:T(128)S(1)}, s32[64]{0:T(128)}, u32[]{:S(2)}) copy-start(s32[64]{0:T(128)} %param.15) | copy-start | bytes 772
  9.0 98.1 %copy-start.5 = (s32[64]{0:T(128)S(1)}, s32[64]{0:T(128)}, u32[]{:S(2)}) copy-start(s32[64]{0:T(128)} %param.14) | copy-start | bytes 772
  9.0 142.0 %copy-start.2 = (bf16[2,128,128]{2,1,0:T(8,128)(2,1)S(1)}, bf16[2,128,128]{2,1,0:T(8,128)(2,1)}, u32[]{:S(2)}) copy-start(bf16[2,128,128]{2,1,0:T(8,128)(2,1)} %param.16) | copy-start | bytes 196612
  9.0 143.0 %copy-start.3 = (bf16[2,64,128]{2,1,0:T(8,128)(2,1)S(1)}, bf16[2,64,128]{2,1,0:T(8,128)(2,1)}, u32[]{:S(2)}) copy-start(bf16[2,64,128]{2,1,0:T(8,128)(2,1)} %param.17) | copy-start | bytes 98308
  10.4 1.2 copy-start.6
  16.5 1.2 copy-start.6
  22.6 1.2 copy-start.6
  28.8 1.2 copy-start.6
  34.9 1.2 copy-start.6
  41.0 1.2 copy-start.6
  47.1 1.2 copy-start.6
  53.2 1.2 copy-start.6
  59.3 1.2 copy-start.6
  65.4 1.2 copy-start.6
  71.6 1.2 copy-start.6
  77.7 1.2 copy-start.6
  83.8 1.2 copy-start.6
  89.9 1.2 copy-start.6
  96.0 1.2 copy-start.6
  102.1 1.2 copy-start.6
  106.9 824.9 %all-reduce.3.cloned.1.call-start = ((), (), s32[]{:S(2)}) async-start(), calls=%async_computation.2 | async-start | bytes 262144 | tf_op jit(solution)/shard_map/psum | solution.py:62
  152.0 781.1 %copy-start.1 = (f32[2,64,128]{2,1,0:T(8,128)}, f32[2,64,128]{2,1,0:T(8,128)S(1)}, u32[]{:S(2)}) copy-start(f32[2,64,128]{2,1,0:T(8,128)S(1)} %fusion.15) | copy-start | bytes 196612
Sparse Core Ops, SparseCore 0:
  107.0 43.9 reduce-scatter.1
  154.2 777.6 all-reduce.2
where the time goes:
time: 941 us; the launch traced here: 940 us
  waiting for transfers between devices  822 us (87%)
  local copies, waits for them, and re-layouts  52.6 us (6%)
  matrix products  30.8 us (3%)
  other arithmetic  19.3 us (2%)
  between operations  14.1 us (1%)
    psum x1, waiting for transfers between devices, local(): summed = lax.psum(local_grad, 'recv')  778 us
    reduce_scatter x1, waiting for transfers between devices, local(): lax.psum_scatter(lax.map(column, (code_pilot, sign_rows.T)), 'sweep', sca...  43.9 us
    dot_general x16, matrix products, column(): jnp.einsum('s,srt->rt', signs_col, records, preferred_element_type=jnp.fl...  20.2 us
    another operation x32, local copies, waits for them, and re-layouts, toeplitz(): jnp.tile(extended, lagcount)[:lagcount * samples].reshape(lagcount, samples)  19.6 us
  transfers between devices with their start and end apart: 2, of which 2 were waited for; matrix products, arithmetic and copies ran while one was open for 0% of the time, Pallas kernels for 0%

commit v1 on v0

v1 whole, which is shorter than its diff:
```python
import functools
import math

import jax
import jax.numpy as jnp
from jax import lax
from jax.experimental import pallas as pl
from jax.experimental.pallas import tpu as pltpu
from jax.sharding import PartitionSpec as P

BF = jnp.bfloat16
F32 = jnp.float32
FINE = 16
LANES = 128


def kernel(
    ns, nr,
    rec_h, pil_h, had_h, cv_h, own_h, live_h, fil_h, tgt_h,
    resp_h, grad_h,
    rec, pil, had, cv, own, live, fil, tgt,
    rect, wmat, xs, sb, rb, wgt, resp, gs, ch, gb, gout,
    in_sem, s1_send, s1_recv, s2_send, s2_recv, out_sem,
):
    me = lax.axis_index("sweep")
    mr = lax.axis_index("recv")
    held, chans, samples = rec.shape
    codes, plen = pil.shape
    lags = fil.shape[1]
    owned = fil.shape[0]
    coarse = lags // FINE
    pairs = coarse // 2
    rows = lags // nr

    pairs_in = [
        (pil_h, pil), (cv_h, cv), (rec_h, rec), (had_h, had),
        (own_h, own), (live_h, live), (fil_h, fil), (tgt_h, tgt),
    ]
    loads = [pltpu.make_async_copy(a, b, in_sem.at[i]) for i, (a, b) in enumerate(pairs_in)]
    for c in loads:
        c.start()
    l_pil, l_cv, l_rec, l_had, l_own, l_live, l_fil, l_tgt = loads

    barrier = pltpu.get_barrier_semaphore()
    for k in range(1, ns):
        pl.semaphore_signal(barrier, inc=1, device_id={"sweep": lax.rem(me + k, ns)},
                            device_id_type=pl.DeviceIdType.MESH)
    @pl.loop(1, nr)
    def _(k):
        pl.semaphore_signal(barrier, inc=1, device_id={"recv": lax.rem(mr + k, nr)},
                            device_id_type=pl.DeviceIdType.MESH)

    l_pil.wait()
    l_cv.wait()
    row = lax.broadcasted_iota(jnp.int32, (codes, codes), 0)
    col = lax.broadcasted_iota(jnp.int32, (codes, codes), 1)
    pick = jnp.zeros((codes, codes), jnp.int32)
    for q in range(codes):
        v = cv[lax.rem(owned * me + q, codes)]
        pick = jnp.where(row == q, v, pick)
    onehot = (pick == col).astype(F32).astype(BF)
    cp = jnp.dot(onehot, pil[...], preferred_element_type=F32)
    cp = jnp.concatenate([cp, jnp.zeros((codes, samples - plen), F32)], axis=1)
    for f in range(FINE):
        shifted = cp if f == 0 else pltpu.roll(cp, f, 1)
        wmat[f * codes:(f + 1) * codes, :] = shifted.astype(BF)

    l_rec.wait()
    for b in range(samples // LANES):
        blk = rec[:, :, b * LANES:(b + 1) * LANES].reshape(held * chans, LANES)
        rect[b * LANES:(b + 1) * LANES, :] = blk.T
    rect[samples:samples + LANES, :] = jnp.zeros((LANES, LANES), BF)

    l_had.wait()
    low = lax.broadcasted_iota(jnp.int32, (1, LANES), 1) < chans
    norm = 1.0 / math.sqrt(codes)
    coef = []
    for q in range(codes):
        c = lax.rem(owned * me + q, codes)
        h0 = had[held * me, c].astype(F32) * norm
        h1 = had[held * me + 1, c].astype(F32) * norm
        coef.append(jnp.where(low, h0, h1))

    l_own.wait()
    l_live.wait()
    own_t = jnp.broadcast_to(own[...].astype(F32), (LANES, chans)).T
    live_t = jnp.broadcast_to(live[...].astype(F32), (LANES, chans)).T
    for c in range(owned):
        v = cv[owned * me + c].astype(F32)
        wgt[c * chans:(c + 1) * chans, :] = live_t * jnp.where(own_t == v, 1.25, 0.25)

    pl.semaphore_wait(barrier, ns - 1 + nr - 1)

    def copy1(k, p):
        return pltpu.make_async_remote_copy(
            src_ref=sb.at[k, pl.ds(2 * FINE * p, 2 * FINE)],
            dst_ref=rb.at[k - 1, pl.ds(2 * FINE * p, 2 * FINE)],
            send_sem=s1_send.at[k - 1, p], recv_sem=s1_recv.at[k - 1, p],
            device_id={"sweep": lax.rem(me + k, ns)}, device_id_type=pl.DeviceIdType.MESH)

    for p in range(pairs):
        base = 2 * FINE * p
        rhs = jnp.concatenate(
            [rect[base:base + samples, :], rect[base + FINE:base + FINE + samples, :]], axis=1)
        acc = jnp.dot(wmat[...], rhs, preferred_element_type=F32)
        xs[p, 0] = acc[:, :LANES]
        xs[p, 1] = acc[:, LANES:]
        for kk in range(ns):
            k = (kk + 1) % ns
            for par in range(2):
                a = xs[p, par, pl.ds(2 * k, FINE, stride=codes), :] * coef[2 * k]
                b = xs[p, par, pl.ds(2 * k + 1, FINE, stride=codes), :] * coef[2 * k + 1]
                part = jnp.where(low, a, b) + pltpu.roll(jnp.where(low, b, a), chans, 1)
                lo = base + par * FINE
                sb[k, lo:lo + FINE, :] = part.astype(BF)
            if k:
                copy1(k, p).start()

    pieces = []
    for p in range(pairs):
        base = 2 * FINE * p
        tot = sb[0, base:base + 2 * FINE, :].astype(F32)
        for k in range(1, ns):
            copy1(k, p).wait_recv()
            tot = tot + rb[k - 1, base:base + 2 * FINE, :].astype(F32)
        pieces.append(tot)
    dec_t32 = jnp.concatenate(pieces, axis=0)
    dec_t = dec_t32.astype(BF)
    dec = dec_t.T
    l_fil.wait()
    l_tgt.wait()
    res = []
    rowid = lax.broadcasted_iota(jnp.int32, (owned * chans, 1), 0)
    for c in range(owned):
        r = jnp.dot(dec[c * chans:(c + 1) * chans, :], fil[c], preferred_element_type=F32)
        resp[c] = r
        res.append(wgt[c * chans:(c + 1) * chans, :] * (r - tgt[c].astype(F32)))
    out1 = pltpu.make_async_copy(resp, resp_h, out_sem.at[0])
    out1.start()
    zero = jnp.zeros((chans, LANES), BF)
    res2 = jnp.concatenate([
        jnp.concatenate([res[0].astype(BF), zero], axis=1),
        jnp.concatenate([zero, res[1].astype(BF)], axis=1)], axis=0)
    g = jnp.dot(dec_t, res2, preferred_element_type=F32)
    for c in range(owned):
        gs[c] = g[:, c * lags:(c + 1) * lags]
    parts = []
    for c in range(owned):
        for i in range(rows):
            parts.append(gs[c, pl.ds(i, nr, stride=rows), :])
    ch[...] = jnp.stack(parts, axis=1).astype(BF)

    def copy2(k):
        j = lax.rem(mr + k, nr)
        return pltpu.make_async_remote_copy(
            src_ref=ch.at[j], dst_ref=gb.at[k], send_sem=s2_send.at[0], recv_sem=s2_recv.at[0],
            device_id={"recv": j}, device_id_type=pl.DeviceIdType.MESH)

    @pl.loop(1, nr)
    def _(k):
        copy2(k).start()

    total = ch[mr].astype(F32)
    for p in range(pairs):
        for k in range(1, ns):
            copy1(k, p).wait_send()
    everything = gb.at[pl.ds(1, nr - 1)]
    pltpu.make_async_copy(everything, everything, s2_recv.at[0]).wait()
    total = total + jnp.sum(gb[pl.ds(1, nr - 1)].astype(F32), axis=0)
    factor = 1.0 / math.sqrt(chans * nr)
    for c in range(owned):
        gout[c] = total[c * rows:(c + 1) * rows, :] * factor
    out2 = pltpu.make_async_copy(gout, grad_h, out_sem.at[1])
    out2.start()
    sent = ch.at[pl.ds(0, nr - 1)]
    pltpu.make_async_copy(sent, sent, s2_send.at[0]).wait()
    out1.wait()
    out2.wait()


def solution(mesh):
    ns, nr = mesh.shape["sweep"], mesh.shape["recv"]

    def local(records, pilots, hadamard, code_vibrator, owner_map, live_mask, filters, targets):
        held, chans, samples = records.shape
        codes, plen = pilots.shape
        owned, lags, _ = filters.shape
        rows = lags // nr
        any_spec = pl.BlockSpec(memory_space=pltpu.HBM)
        vm = pltpu.VMEM
        return pl.pallas_call(
            functools.partial(kernel, ns, nr),
            out_shape=(
                jax.ShapeDtypeStruct((owned, chans, lags), F32),
                jax.ShapeDtypeStruct((owned, rows, lags), F32),
            ),
            in_specs=[any_spec] * 8,
            out_specs=(any_spec, any_spec),
            scratch_shapes=[
                vm((held, chans, samples), BF), vm((codes, plen), BF),
                pltpu.SMEM((codes, codes), jnp.int32), pltpu.SMEM((codes,), jnp.int32),
                vm((1, chans), jnp.int32), vm((1, chans), jnp.int32),
                vm((owned, lags, lags), BF), vm((owned, chans, lags), BF),
                vm((samples + LANES, LANES), BF), vm((FINE * codes, samples), BF),
                vm((lags // FINE // 2, 2, FINE * codes, LANES), F32),
                vm((ns, lags, LANES), BF), vm((ns - 1, lags, LANES), BF),
                vm((owned * chans, LANES), F32), vm((owned, chans, lags), F32),
                vm((owned, lags, lags), F32),
                vm((nr, owned * rows, lags), BF), vm((nr, owned * rows, lags), BF),
                vm((owned, rows, lags), F32),
                pltpu.SemaphoreType.DMA((8,)),
                pltpu.SemaphoreType.DMA((ns - 1, lags // FINE // 2)),
                pltpu.SemaphoreType.DMA((ns - 1, lags // FINE // 2)),
                pltpu.SemaphoreType.DMA((1,)), pltpu.SemaphoreType.DMA((1,)),
                pltpu.SemaphoreType.DMA((2,)),
            ],
            compiler_params=pltpu.CompilerParams(
                collective_id=0, has_side_effects=True, vmem_limit_bytes=64 * 1024 * 1024),
        )(records, pilots, hadamard, code_vibrator, owner_map.reshape(1, -1),
          live_mask.reshape(1, -1), filters, targets)

    in_specs = (
        P("sweep", "recv", None), P(), P(), P(), P("recv"), P("recv"),
        P("sweep", None, None), P("sweep", "recv", None),
    )
    out_specs = (P("sweep", "recv", None), P("sweep", "recv", None))
    return jax.shard_map(local, mesh=mesh, in_specs=in_specs, out_specs=out_specs, check_vma=False)
```

time: 941 us -> 38.5 us (0.04)
  the two profiles are of different devices: /device:TPU:8 before, /device:TPU:1 now
where the time goes in v1:
time: 38.5 us; the launch traced here: 38.3 us
  Pallas kernels  35.6 us (92%)
  local copies, waits for them, and re-layouts  2.06 us (5%)
  between operations  0.65 us (2%)
    pallas_call x1, Pallas kernels, local(): pl.pallas_call(functools.partial(kernel, ns, nr), out_shape=(jax.ShapeDty...  35.6 us
    unnamed x4, local copies, waits for them, and re-layouts  2.06 us

profile of v1, /device:TPU:1, one launch (start us, length us, event | category | flops | bytes accessed | tf_op | source)
XLA Modules:
  0.0 38.3 jit_solution(12795104024106480470)
XLA Ops:
  0.6 35.6 %shard_map.95 = (f32[2,64,128]{2,1,0:T(8,128)}, f32[2,2,128]{2,1,0:T(2,128)}) custom-call(bf16[2,64,4096]{2,1,0:T(8,128)(2,1)} %rec_h.1, bf16[16,3968]{1,0:T(8,128)(2,1)} %pil_h.1, s32[16,16]{1,0:T(8,128)} %had_h.1, s32[16]{0:T(128)} %cv_h.1, s32[1,64]{1,0:T(1,128)} %bitcast.2, s32[1,64]{1,0:T(1,128)} %bitcast.3, bf16[2,128,128]{2,1,0:T(8,128)(2,1)} %fil_h.1, ...), custom_call_target="tpu_custom_call" | custom-call | tf_op jit(solution)/shard_map/pallas_call | solution.py:191
  36.2 0.0 copy-start
  36.2 1.5 %copy.12 = f32[2,64,128]{2,1,0:T(8,128)} copy(f32[2,64,128]{2,1,0:T(8,128)} %get-tuple-element.4) | data formatting | bytes 131072
  37.7 0.0 copy-done
  37.7 0.6 %copy.13 = f32[2,2,128]{2,1,0:T(2,128)} copy(f32[2,2,128]{2,1,0:T(2,128)S(1)} %copy-done) | data formatting | bytes 4096
Async XLA Ops:
  36.2 1.5 %copy-start = (f32[2,2,128]{2,1,0:T(2,128)S(1)}, f32[2,2,128]{2,1,0:T(2,128)}, u32[]{:S(2)}) copy-start(f32[2,2,128]{2,1,0:T(2,128)} %get-tuple-element.5) | copy-start | bytes 6148

commit v2 on v1

v2 whole, which is shorter than its diff:
```python
import functools
import math

import jax
import jax.numpy as jnp
from jax import lax
from jax.experimental import pallas as pl
from jax.experimental.pallas import tpu as pltpu
from jax.sharding import PartitionSpec as P

BF = jnp.bfloat16
F32 = jnp.float32
FINE = 16
LANES = 128
GROUP = 2
PARTS = 4
MESH = pl.DeviceIdType.MESH


def cube(nr):
    return (4, 8, 2) if nr == 64 else (1, nr // 2, 2)


def kernel(
    ns, nr,
    rec_h, pil_h, had_h, cv_h, own_h, live_h, fil_h, tgt_h,
    resp, grad,
    rec, pil, had, cv, own, live, fil, tgt,
    rect, wmat, xs, sb, rb, wgt, gs, ch, gb,
    in_sem, rec_sem, sib_send, sib_recv, s1_send, s1_recv, s2_send, s2_recv, relay,
):
    me = lax.axis_index("sweep")
    mr = lax.axis_index("recv")
    _, held, half, samples = rec.shape
    chans = 2 * half
    codes, plen = pil.shape
    lags = fil.shape[1]
    owned = fil.shape[0]
    pairs = lags // FINE // 2
    rows = lags // nr
    nx, ny, nz = cube(nr)
    x, y, z = mr // (ny * nz), mr // nz % ny, mr % nz
    core = me % 2
    bits = (me // 4, me // 2 % 2, core)

    def mate(k):
        a, b, c = [1 - v if k >> (2 - i) & 1 else v for i, v in enumerate(bits)]
        return a * 4 + b * 2 + c

    def at(dx, dy, dz):
        return ((x + dx) % nx * ny + (y + dy) % ny) * nz + (z + dz) % nz

    sib = mate(1)
    order = [6, 7, 4, 5, 2, 3, 1]

    part = samples // PARTS
    mine = pl.ds(pl.multiple_of(core * half, half), half)
    theirs = pl.ds(pl.multiple_of((1 - core) * half, half), half)
    small = [(pil_h, pil), (cv_h, cv), (had_h, had), (own_h, own), (live_h, live), (fil_h, fil), (tgt_h, tgt)]
    loads = [pltpu.make_async_copy(a, b, in_sem.at[i]) for i, (a, b) in enumerate(small)]
    own_rec = [
        pltpu.make_async_copy(
            rec_h.at[:, mine, pl.ds(i * part, part)], rec.at[0, :, :, pl.ds(i * part, part)], rec_sem.at[i])
        for i in range(PARTS)
    ]
    l_pil, l_cv, l_had, l_own, l_live, l_fil, l_tgt = loads
    l_pil.start()
    l_cv.start()
    for c in own_rec:
        c.start()
    for c in loads[2:]:
        c.start()

    barrier = pltpu.get_barrier_semaphore()
    greet = [{"sweep": mate(k)} for k in [1] + order[:-1]]
    ys = [{"recv": at(0, d, 0)} for d in range(1, ny)]
    zs = [{"recv": at(0, 0, d)} for d in range(1, nz)]
    greet += ys + zs + [{"recv": at(d, 0, 0)} for d in range(1, nx)]
    for d in greet:
        pl.semaphore_signal(barrier, inc=1, device_id=d, device_id_type=MESH)

    l_pil.wait()
    l_cv.wait()
    slot_code = [owned * mate(k) + i for k in range(ns) for i in range(owned)]
    row = lax.broadcasted_iota(jnp.int32, (codes, codes), 0)
    col = lax.broadcasted_iota(jnp.int32, (codes, codes), 1)
    pick = jnp.zeros((codes, codes), jnp.int32)
    for q in range(codes):
        pick = jnp.where(row == q, cv[slot_code[q]], pick)
    onehot = (pick == col).astype(F32).astype(BF)
    cp = jnp.dot(onehot, pil[...], preferred_element_type=F32)
    cp = jnp.concatenate([cp, jnp.zeros((codes, samples - plen), F32)], axis=1)
    for f in range(FINE):
        shifted = cp if f == 0 else pltpu.roll(cp, f, 1)
        wmat[f * codes:(f + 1) * codes, :] = shifted.astype(BF)

    pl.semaphore_wait(barrier, len(greet))
    trade = [
        pltpu.make_async_remote_copy(
            src_ref=rec_h.at[:, theirs, pl.ds(i * part, part)],
            dst_ref=rec.at[1, :, :, pl.ds(i * part, part)],
            send_sem=sib_send.at[i], recv_sem=sib_recv.at[i],
            device_id={"sweep": sib}, device_id_type=MESH)
        for i in range(PARTS)
    ]
    for c in trade:
        c.start()
    for d in ys:
        pl.semaphore_signal(relay.at[0], inc=1, device_id=d, device_id_type=MESH)

    lane = lax.broadcasted_iota(jnp.int32, (1, LANES), 1)
    group = lane // half
    l_had.wait()
    norm = 1.0 / math.sqrt(codes)
    sweeps = [held * me + i for i in range(held)] + [held * sib + i for i in range(held)]
    coef = []
    for q in range(codes):
        v = jnp.zeros((1, LANES), F32)
        for g, s in enumerate(sweeps):
            v = jnp.where(group == g, had[s, slot_code[q]].astype(F32) * norm, v)
        coef.append(v)
    l_own.wait()
    l_live.wait()
    own_t = jnp.broadcast_to(own[...].astype(F32), (LANES, chans)).T
    live_t = jnp.broadcast_to(live[...].astype(F32), (LANES, chans)).T
    for c in range(owned):
        v = cv[owned * me + c].astype(F32)
        wgt[c * chans:(c + 1) * chans, :] = live_t * jnp.where(own_t == v, 1.25, 0.25)

    rect[samples:samples + LANES, :] = jnp.zeros((LANES, LANES), BF)
    for i in range(PARTS):
        own_rec[i].wait()
        trade[i].wait_recv()
        for b in range(i * part // LANES, (i + 1) * part // LANES):
            blk = rec[:, :, :, b * LANES:(b + 1) * LANES].reshape(2 * held * half, LANES)
            rect[b * LANES:(b + 1) * LANES, :] = blk.T

    def copy1(k, p):
        return pltpu.make_async_remote_copy(
            src_ref=sb.at[k, pl.ds(p * GROUP, GROUP)], dst_ref=rb.at[k - 1, pl.ds(p * GROUP, GROUP)],
            send_sem=s1_send.at[k - 1, p], recv_sem=s1_recv.at[k - 1, p],
            device_id={"sweep": mate(k)}, device_id_type=MESH)

    low = group < 2
    outer = (group == 0) | (group == 3)
    even = group % 2 == 0
    def correlate(p):
        base = 2 * FINE * p
        rhs = jnp.concatenate(
            [rect[base:base + samples, :], rect[base + FINE:base + FINE + samples, :]], axis=1)
        acc = jnp.dot(wmat[...], rhs, preferred_element_type=F32)
        xs[p, 0] = acc[:, :LANES]
        xs[p, 1] = acc[:, LANES:]

    def decode(p):
        for k in order + [0]:
            a0, b0, a1, b1 = [
                xs[p, par, pl.ds(2 * k + i, FINE, stride=codes), :] * coef[2 * k + i]
                for par in range(2) for i in range(2)
            ]
            u = jnp.where(low, b0, b1) + pltpu.roll(jnp.where(low, b1, b0), 2 * half, 1)
            v = jnp.where(outer, a0, a1) + pltpu.roll(jnp.where(outer, a1, a0), 2 * half, 1)
            t = jnp.where(even, v, u) + pltpu.roll(jnp.where(even, u, v), half, 1)
            sb[k, p] = t.astype(BF)

    for p in range(pairs):
        correlate(p)
        decode(p)
        if p % GROUP == GROUP - 1:
            for k in order:
                copy1(k, p // GROUP).start()

    pl.semaphore_wait(relay.at[0], ny - 1)
    for d in zs:
        pl.semaphore_signal(relay.at[1], inc=1, device_id=d, device_id_type=MESH)

    first = jnp.full((FINE, LANES), core, jnp.int32) == 0
    pieces = []
    for p in range(pairs):
        if p % GROUP == 0:
            for k in order:
                copy1(k, p // GROUP).wait_recv()
        here = sb[0, p].astype(F32)
        for k in (6, 4, 2):
            here = here + rb[k - 1, p].astype(F32)
        there = None
        for k in (7, 5, 3, 1):
            v = rb[k - 1, p].astype(F32)
            there = v if there is None else there + v
        h0 = jnp.where(first, here, there)
        h1 = jnp.where(first, there, here)
        pieces.append(jnp.where(low, h0, pltpu.roll(h1, 2 * half, 1)))
        pieces.append(jnp.where(low, pltpu.roll(h0, 2 * half, 1), h1))
    dec_t = jnp.concatenate(pieces, axis=0).astype(BF)
    dec = dec_t.T
    l_fil.wait()
    l_tgt.wait()
    res = []
    for c in range(owned):
        lhs = jnp.concatenate([dec[(h * owned + c) * half:(h * owned + c + 1) * half, :] for h in range(2)], axis=0)
        r = jnp.dot(lhs, fil[c], preferred_element_type=F32)
        resp[c] = r
        res.append((wgt[c * chans:(c + 1) * chans, :] * (r - tgt[c].astype(F32))).astype(BF))
    zero = jnp.zeros((half, lags), BF)
    blocks = []
    for h in range(2):
        for c in range(owned):
            blocks.append(jnp.concatenate(
                [res[c][h * half:(h + 1) * half, :] if e == c else zero for e in range(owned)], axis=1))
    g = jnp.dot(dec_t, jnp.concatenate(blocks, axis=0), preferred_element_type=F32)
    for c in range(owned):
        gs[c] = g[:, c * lags:(c + 1) * lags]
    ch[...] = jnp.stack(
        [gs[c, pl.ds(i, nr, stride=rows), :] for c in range(owned) for i in range(rows)], axis=1).astype(BF)

    steps = [(dx, dy, dz) for dx in range(nx) for dy in range(ny) for dz in range(nz)]
    steps.sort(key=lambda s: -(min(s[0], nx - s[0]) + min(s[1], ny - s[1]) + 4 * s[2]))
    pl.semaphore_wait(relay.at[1], nz - 1)
    for n, s in enumerate(steps[:-1]):
        j = at(*s)
        pltpu.make_async_remote_copy(
            src_ref=ch.at[j], dst_ref=gb.at[n], send_sem=s2_send.at[0], recv_sem=s2_recv.at[0],
            device_id={"recv": j}, device_id_type=MESH).start()

    total = ch[mr].astype(F32)
    for c in trade:
        c.wait_send()
    for p in range(pairs // GROUP):
        for k in order:
            copy1(k, p).wait_send()
    sent = ch.at[pl.ds(0, nr - 1)]
    pltpu.make_async_copy(sent, sent, s2_send.at[0]).wait()
    pltpu.make_async_copy(gb, gb, s2_recv.at[0]).wait()
    total = total + jnp.sum(gb[...].astype(F32), axis=0)
    factor = 1.0 / math.sqrt(chans * nr)
    for c in range(owned):
        grad[c] = total[c * rows:(c + 1) * rows, :] * factor


def solution(mesh):
    ns, nr = mesh.shape["sweep"], mesh.shape["recv"]

    def local(records, pilots, hadamard, code_vibrator, owner_map, live_mask, filters, targets):
        held, chans, samples = records.shape
        codes, plen = pilots.shape
        owned, lags, _ = filters.shape
        rows = lags // nr
        pairs = lags // FINE // 2
        vm = pltpu.VMEM
        dma = pltpu.SemaphoreType.DMA
        operands = (records, pilots, hadamard, code_vibrator, owner_map.reshape(1, -1),
                    live_mask.reshape(1, -1), filters, targets)
        return pl.pallas_call(
            functools.partial(kernel, ns, nr),
            out_shape=(vm((owned, chans, lags), F32), vm((owned, rows, lags), F32)),
            in_specs=[pl.BlockSpec(memory_space=pltpu.HBM)] * 8,
            out_specs=(pl.BlockSpec(memory_space=vm),) * 2,
            scratch_shapes=[
                vm((2, held, chans // 2, samples), BF), vm((codes, plen), BF),
                pltpu.SMEM((codes, codes), jnp.int32), pltpu.SMEM((codes,), jnp.int32),
                vm((1, chans), jnp.int32), vm((1, chans), jnp.int32),
                vm((owned, lags, lags), BF), vm((owned, chans, lags), BF),
                vm((samples + LANES, LANES), BF), vm((FINE * codes, samples), BF),
                vm((pairs, 2, FINE * codes, LANES), F32),
                vm((ns, pairs, FINE, LANES), BF), vm((ns - 1, pairs, FINE, LANES), BF),
                vm((owned * chans, lags), F32), vm((owned, lags, lags), F32),
                vm((nr, owned * rows, lags), BF), vm((nr - 1, owned * rows, lags), BF),
                dma((7,)), dma((PARTS,)), dma((PARTS,)), dma((PARTS,)),
                dma((ns - 1, pairs // GROUP)), dma((ns - 1, pairs // GROUP)), dma((1,)), dma((1,)),
                pltpu.SemaphoreType.REGULAR((2,)),
            ],
            compiler_params=pltpu.CompilerParams(
                collective_id=0, has_side_effects=True, vmem_limit_bytes=40 * 1024 * 1024),
        )(*[pltpu.with_memory_space_constraint(a, pltpu.HBM) for a in operands])

    in_specs = (
        P("sweep", "recv", None), P(), P(), P(), P("recv"), P("recv"),
        P("sweep", None, None), P("sweep", "recv", None),
    )
    out_specs = (P("sweep", "recv", None), P("sweep", "recv", None))
    return jax.shard_map(local, mesh=mesh, in_specs=in_specs, out_specs=out_specs, check_vma=False)
```

time: 38.5 us -> 33.6 us (0.87)
  Pallas kernels: 35.6 us -> 31.6 us
  local copies, waits for them, and re-layouts: 2.06 us -> 1.21 us
    pallas_call x1, Pallas kernels: 35.6 us -> 31.6 us  [local(): pl.pallas_call(functools.partial(kernel, ns, nr), out_shape=(vm((owned, c...]
    unnamed x4 -> x2, local copies, waits for them, and re-layouts: 2.06 us -> 1.21 us
where the time goes in v2:
time: 33.6 us; the launch traced here: 33.4 us
  Pallas kernels  31.6 us (94%)
  local copies, waits for them, and re-layouts  1.21 us (4%)
  between operations  0.64 us (2%)
    pallas_call x1, Pallas kernels, local(): pl.pallas_call(functools.partial(kernel, ns, nr), out_shape=(vm((owned, c...  31.6 us
    unnamed x2, local copies, waits for them, and re-layouts  1.21 us

profile of v2, /device:TPU:1, one launch (start us, length us, event | category | flops | bytes accessed | tf_op | source)
XLA Modules:
  0.0 33.4 jit_solution(16931519382732394462)
XLA Ops:
  0.6 31.6 %shard_map.95 = (f32[2,64,128]{2,1,0:T(8,128)S(1)}, f32[2,2,128]{2,1,0:T(2,128)S(1)}) custom-call(bf16[2,64,4096]{2,1,0:T(8,128)(2,1)} %rec_h.1, bf16[16,3968]{1,0:T(8,128)(2,1)} %pil_h.1, s32[16,16]{1,0:T(8,128)} %had_h.1, s32[16]{0:T(128)} %cv_h.1, s32[1,64]{1,0:T(1,128)} %bitcast.2, s32[1,64]{1,0:T(1,128)} %bitcast.3, bf16[2,128,128]{2,1,0:T(8,128)(2,1)} %fil_h.1, ...), custom_call_target="tpu_custom_call" | custom-call | tf_op jit(solution)/shard_map/pallas_call | solution.py:253
  32.2 0.6 %copy.12 = f32[2,64,128]{2,1,0:T(8,128)} copy(f32[2,64,128]{2,1,0:T(8,128)S(1)} %get-tuple-element.2) | data formatting | bytes 131072
  32.9 0.6 %copy.13 = f32[2,2,128]{2,1,0:T(2,128)} copy(f32[2,2,128]{2,1,0:T(2,128)S(1)} %get-tuple-element.3) | data formatting | bytes 4096

commit v3 on v2

--- a/solution.py
+++ b/solution.py
@@ -10,9 +10,9 @@
 
 BF = jnp.bfloat16
 F32 = jnp.float32
-FINE = 16
+FINE = 32
 LANES = 128
-GROUP = 2
+SIDES = 2
 PARTS = 4
 MESH = pl.DeviceIdType.MESH
 
@@ -27,7 +27,7 @@
     resp, grad,
     rec, pil, had, cv, own, live, fil, tgt,
     rect, wmat, xs, sb, rb, wgt, gs, ch, gb,
-    in_sem, rec_sem, sib_send, sib_recv, s1_send, s1_recv, s2_send, s2_recv, relay,
+    in_sem, rec_sem, sib_send, sib_recv, s1_send, s1_recv, s2_send, s2_recv, pair, relay,
 ):
     me = lax.axis_index("sweep")
     mr = lax.axis_index("recv")
@@ -51,7 +51,9 @@
         return ((x + dx) % nx * ny + (y + dy) % ny) * nz + (z + dz) % nz
 
     sib = mate(1)
-    order = [6, 7, 4, 5, 2, 3, 1]
+    order = [[6, 7, 4, 5], [2, 3, 1]]
+    ranks = ns // SIDES
+    slots = codes // SIDES
 
     part = samples // PARTS
     mine = pl.ds(pl.multiple_of(core * half, half), half)
@@ -72,12 +74,42 @@
         c.start()
 
     barrier = pltpu.get_barrier_semaphore()
-    greet = [{"sweep": mate(k)} for k in [1] + order[:-1]]
     ys = [{"recv": at(0, d, 0)} for d in range(1, ny)]
     zs = [{"recv": at(0, 0, d)} for d in range(1, nz)]
+    greet = [{"sweep": mate(k)} for k in range(2, ns, 2)]
     greet += ys + zs + [{"recv": at(d, 0, 0)} for d in range(1, nx)]
-    for d in greet:
-        pl.semaphore_signal(barrier, inc=1, device_id=d, device_id_type=MESH)
+
+    def tell(sem, device):
+        pl.semaphore_signal(sem, inc=1, device_id=device, device_id_type=MESH)
+
+    @pl.when(core == 1)
+    def _():
+        tell(barrier, {"sweep": sib})
+
+    @pl.when(core == 0)
+    def _():
+        pl.semaphore_wait(barrier, 1)
+        tell(pair.at[0], {"sweep": sib})
+
+    @pl.when(core == 1)
+    def _():
+        pl.semaphore_wait(pair.at[0], 1)
+
+    trade = [
+        pltpu.make_async_remote_copy(
+            src_ref=rec_h.at[:, theirs, pl.ds(i * part, part)],
+            dst_ref=rec.at[1, :, :, pl.ds(i * part, part)],
+            send_sem=sib_send.at[i], recv_sem=sib_recv.at[i],
+            device_id={"sweep": sib}, device_id_type=MESH)
+        for i in range(PARTS)
+    ]
+    for c in trade:
+        c.start()
+
+    @pl.when(core == 1)
+    def _():
+        for d in greet:
+            tell(barrier, d)
 
     l_pil.wait()
     l_cv.wait()
@@ -90,23 +122,12 @@
     onehot = (pick == col).astype(F32).astype(BF)
     cp = jnp.dot(onehot, pil[...], preferred_element_type=F32)
     cp = jnp.concatenate([cp, jnp.zeros((codes, samples - plen), F32)], axis=1)
-    for f in range(FINE):
-        shifted = cp if f == 0 else pltpu.roll(cp, f, 1)
-        wmat[f * codes:(f + 1) * codes, :] = shifted.astype(BF)
-
-    pl.semaphore_wait(barrier, len(greet))
-    trade = [
-        pltpu.make_async_remote_copy(
-            src_ref=rec_h.at[:, theirs, pl.ds(i * part, part)],
-            dst_ref=rec.at[1, :, :, pl.ds(i * part, part)],
-            send_sem=sib_send.at[i], recv_sem=sib_recv.at[i],
-            device_id={"sweep": sib}, device_id_type=MESH)
-        for i in range(PARTS)
-    ]
-    for c in trade:
-        c.start()
-    for d in ys:
-        pl.semaphore_signal(relay.at[0], inc=1, device_id=d, device_id_type=MESH)
+    for f in range(0, FINE, 2):
+        a = cp if f == 0 else pltpu.roll(cp, f, 1)
+        b = pltpu.roll(cp, f + 1, 1)
+        for g in range(SIDES):
+            both = jnp.concatenate([a[g * slots:(g + 1) * slots], b[g * slots:(g + 1) * slots]], axis=0)
+            wmat[g, f * slots:(f + 2) * slots, :] = both.astype(BF)
 
     lane = lax.broadcasted_iota(jnp.int32, (1, LANES), 1)
     group = lane // half
@@ -135,58 +156,71 @@
             blk = rec[:, :, :, b * LANES:(b + 1) * LANES].reshape(2 * held * half, LANES)
             rect[b * LANES:(b + 1) * LANES, :] = blk.T
 
-    def copy1(k, p):
+    def copy1(k):
         return pltpu.make_async_remote_copy(
-            src_ref=sb.at[k, pl.ds(p * GROUP, GROUP)], dst_ref=rb.at[k - 1, pl.ds(p * GROUP, GROUP)],
-            send_sem=s1_send.at[k - 1, p], recv_sem=s1_recv.at[k - 1, p],
+            src_ref=sb.at[k], dst_ref=rb.at[k - 1],
+            send_sem=s1_send.at[k - 1], recv_sem=s1_recv.at[k - 1],
             device_id={"sweep": mate(k)}, device_id_type=MESH)
 
     low = group < 2
     outer = (group == 0) | (group == 3)
     even = group % 2 == 0
-    def correlate(p):
+    def correlate(g, p):
         base = 2 * FINE * p
         rhs = jnp.concatenate(
             [rect[base:base + samples, :], rect[base + FINE:base + FINE + samples, :]], axis=1)
-        acc = jnp.dot(wmat[...], rhs, preferred_element_type=F32)
-        xs[p, 0] = acc[:, :LANES]
-        xs[p, 1] = acc[:, LANES:]
-
-    def decode(p):
-        for k in order + [0]:
-            a0, b0, a1, b1 = [
-                xs[p, par, pl.ds(2 * k + i, FINE, stride=codes), :] * coef[2 * k + i]
-                for par in range(2) for i in range(2)
-            ]
-            u = jnp.where(low, b0, b1) + pltpu.roll(jnp.where(low, b1, b0), 2 * half, 1)
-            v = jnp.where(outer, a0, a1) + pltpu.roll(jnp.where(outer, a1, a0), 2 * half, 1)
-            t = jnp.where(even, v, u) + pltpu.roll(jnp.where(even, u, v), half, 1)
-            sb[k, p] = t.astype(BF)
-
-    for p in range(pairs):
-        correlate(p)
-        decode(p)
-        if p % GROUP == GROUP - 1:
-            for k in order:
-                copy1(k, p // GROUP).start()
+        acc = jnp.dot(wmat[g], rhs, preferred_element_type=F32)
+        xs[g, p, 0] = acc[:, :LANES]
+        xs[g, p, 1] = acc[:, LANES:]
+
+    def decode(g, p, k):
+        q = owned * (k % ranks)
+        a0, b0, a1, b1 = [
+            xs[g, p, par, pl.ds(q + i, FINE, stride=slots), :] * coef[owned * k + i]
+            for par in range(2) for i in range(owned)
+        ]
+        u = jnp.where(low, b0, b1) + pltpu.roll(jnp.where(low, b1, b0), 2 * half, 1)
+        v = jnp.where(outer, a0, a1) + pltpu.roll(jnp.where(outer, a1, a0), 2 * half, 1)
+        t = jnp.where(even, v, u) + pltpu.roll(jnp.where(even, u, v), half, 1)
+        sb[k, p] = t.astype(BF)
+
+    for g in (1, 0):
+        for p in range(pairs):
+            correlate(g, p)
+            for k in range(g * ranks, (g + 1) * ranks):
+                decode(g, p, k)
+        if g == 1:
+            @pl.when(core == 1)
+            def _():
+                pl.semaphore_wait(barrier, len(greet))
+                tell(pair.at[1], {"sweep": sib})
+
+            @pl.when(core == 0)
+            def _():
+                pl.semaphore_wait(pair.at[1], 1)
+
+        for k in order[1 - g]:
+            copy1(k).start()
+        if g == 1:
+            for d in ys:
+                tell(relay.at[0], d)
 
     pl.semaphore_wait(relay.at[0], ny - 1)
     for d in zs:
-        pl.semaphore_signal(relay.at[1], inc=1, device_id=d, device_id_type=MESH)
+        tell(relay.at[1], d)
 
     first = jnp.full((FINE, LANES), core, jnp.int32) == 0
     pieces = []
+    for ks in order:
+        for k in ks:
+            copy1(k).wait_recv()
     for p in range(pairs):
-        if p % GROUP == 0:
-            for k in order:
-                copy1(k, p // GROUP).wait_recv()
         here = sb[0, p].astype(F32)
         for k in (6, 4, 2):
             here = here + rb[k - 1, p].astype(F32)
-        there = None
-        for k in (7, 5, 3, 1):
-            v = rb[k - 1, p].astype(F32)
-            there = v if there is None else there + v
+        there = rb[6, p].astype(F32)
+        for k in (5, 3, 1):
+            there = there + rb[k - 1, p].astype(F32)
         h0 = jnp.where(first, here, there)
         h1 = jnp.where(first, there, here)
         pieces.append(jnp.where(low, h0, pltpu.roll(h1, 2 * half, 1)))
@@ -225,9 +259,9 @@
     total = ch[mr].astype(F32)
     for c in trade:
         c.wait_send()
-    for p in range(pairs // GROUP):
-        for k in order:
-            copy1(k, p).wait_send()
+    for ks in order:
+        for k in ks:
+            copy1(k).wait_send()
     sent = ch.at[pl.ds(0, nr - 1)]
     pltpu.make_async_copy(sent, sent, s2_send.at[0]).wait()
     pltpu.make_async_copy(gb, gb, s2_recv.at[0]).wait()
@@ -235,6 +269,14 @@
     factor = 1.0 / math.sqrt(chans * nr)
     for c in range(owned):
         grad[c] = total[c * rows:(c + 1) * rows, :] * factor
+
+
+def deliver(resp_v, grad_v, resp_h, grad_h, sem):
+    outs = [pltpu.make_async_copy(resp_v, resp_h, sem.at[0]), pltpu.make_async_copy(grad_v, grad_h, sem.at[1])]
+    for c in outs:
+        c.start()
+    for c in outs:
+        c.wait()
 
 
 def solution(mesh):
@@ -250,7 +292,7 @@
         dma = pltpu.SemaphoreType.DMA
         operands = (records, pilots, hadamard, code_vibrator, owner_map.reshape(1, -1),
                     live_mask.reshape(1, -1), filters, targets)
-        return pl.pallas_call(
+        outs = pl.pallas_call(
             functools.partial(kernel, ns, nr),
             out_shape=(vm((owned, chans, lags), F32), vm((owned, rows, lags), F32)),
             in_specs=[pl.BlockSpec(memory_space=pltpu.HBM)] * 8,
@@ -260,18 +302,26 @@
                 pltpu.SMEM((codes, codes), jnp.int32), pltpu.SMEM((codes,), jnp.int32),
                 vm((1, chans), jnp.int32), vm((1, chans), jnp.int32),
                 vm((owned, lags, lags), BF), vm((owned, chans, lags), BF),
-                vm((samples + LANES, LANES), BF), vm((FINE * codes, samples), BF),
-                vm((pairs, 2, FINE * codes, LANES), F32),
+                vm((samples + LANES, LANES), BF), vm((SIDES, FINE * codes // SIDES, samples), BF),
+                vm((SIDES, pairs, 2, FINE * codes // SIDES, LANES), F32),
                 vm((ns, pairs, FINE, LANES), BF), vm((ns - 1, pairs, FINE, LANES), BF),
                 vm((owned * chans, lags), F32), vm((owned, lags, lags), F32),
                 vm((nr, owned * rows, lags), BF), vm((nr - 1, owned * rows, lags), BF),
                 dma((7,)), dma((PARTS,)), dma((PARTS,)), dma((PARTS,)),
-                dma((ns - 1, pairs // GROUP)), dma((ns - 1, pairs // GROUP)), dma((1,)), dma((1,)),
-                pltpu.SemaphoreType.REGULAR((2,)),
+                dma((ns - 1,)), dma((ns - 1,)), dma((1,)), dma((1,)),
+                pltpu.SemaphoreType.REGULAR((2,)), pltpu.SemaphoreType.REGULAR((2,)),
             ],
             compiler_params=pltpu.CompilerParams(
                 collective_id=0, has_side_effects=True, vmem_limit_bytes=40 * 1024 * 1024),
         )(*[pltpu.with_memory_space_constraint(a, pltpu.HBM) for a in operands])
+        hbm = pl.BlockSpec(memory_space=pltpu.HBM)
+        return pl.pallas_call(
+            deliver,
+            out_shape=[jax.ShapeDtypeStruct(a.shape, a.dtype) for a in outs],
+            in_specs=[pl.BlockSpec(memory_space=pl.ANY)] * 2,
+            out_specs=[hbm, hbm],
+            scratch_shapes=[dma((2,))],
+        )(*[pltpu.with_memory_space_constraint(a, vm) for a in outs])
 
     in_specs = (
         P("sweep", "recv", None), P(), P(), P(), P("recv"), P("recv"),

time: 33.6 us -> 31.7 us (0.943)
  local copies, waits for them, and re-layouts: 1.21 us -> 0 us
  Pallas kernels: 31.6 us -> 30.9 us
    pallas_call x1, Pallas kernels: 31.6 us -> 30.3 us  [local(): pl.pallas_call(functools.partial(kernel, ns, nr), out_shape=(vm((owned, c...]
    unnamed x2 -> x0, local copies, waits for them, and re-layouts: 1.21 us -> none
    pallas_call x0 -> x1, Pallas kernels: none -> 0.65 us  [local(): pl.pallas_call(deliver, out_shape=[jax.ShapeDtypeStruct(a.shape, a.dtype)...]
where the time goes in v3:
time: 31.7 us; the launch traced here: 31.6 us
  Pallas kernels  30.9 us (97%)
  between operations  0.64 us (2%)
    pallas_call x1, Pallas kernels, local(): pl.pallas_call(functools.partial(kernel, ns, nr), out_shape=(vm((owned, c...  30.3 us
    pallas_call x1, Pallas kernels, local(): pl.pallas_call(deliver, out_shape=[jax.ShapeDtypeStruct(a.shape, a.dtype)...  0.65 us

profile of v3, /device:TPU:1, one launch (start us, length us, event | category | flops | bytes accessed | tf_op | source)
XLA Modules:
  0.0 31.6 jit_solution(5445292206078929889)
XLA Ops:
  0.6 30.3 %shard_map.95 = (f32[2,64,128]{2,1,0:T(8,128)S(1)}, f32[2,2,128]{2,1,0:T(2,128)S(1)}) custom-call(bf16[2,64,4096]{2,1,0:T(8,128)(2,1)} %rec_h.1, bf16[16,3968]{1,0:T(8,128)(2,1)} %pil_h.1, s32[16,16]{1,0:T(8,128)} %had_h.1, s32[16]{0:T(128)} %cv_h.1, s32[1,64]{1,0:T(1,128)} %bitcast.2, s32[1,64]{1,0:T(1,128)} %bitcast.3, bf16[2,128,128]{2,1,0:T(8,128)(2,1)} %fil_h.1, ...), custom_call_target="tpu_custom_call" | custom-call | tf_op jit(solution)/shard_map/pallas_call | solution.py:295
  30.9 0.7 %shard_map.96 = (f32[2,64,128]{2,1,0:T(8,128)}, f32[2,2,128]{2,1,0:T(2,128)}) custom-call(f32[2,64,128]{2,1,0:T(8,128)S(1)} %get-tuple-element.4.resp_v, f32[2,2,128]{2,1,0:T(2,128)S(1)} %get-tuple-element.5.grad_v), custom_call_target="tpu_custom_call" | custom-call | tf_op jit(solution)/shard_map/pallas_call | solution.py:318

commit v4 on v3

--- a/solution.py
+++ b/solution.py
@@ -13,7 +13,7 @@
 FINE = 32
 LANES = 128
 SIDES = 2
-PARTS = 4
+PARTS = 2
 MESH = pl.DeviceIdType.MESH
 
 
@@ -55,6 +55,19 @@
     ranks = ns // SIDES
     slots = codes // SIDES
 
+    barrier = pltpu.get_barrier_semaphore()
+    ys = [{"recv": at(0, d, 0)} for d in sorted(range(1, ny), key=lambda d: -min(d, ny - d))]
+    zs = [{"recv": at(0, 0, d)} for d in range(1, nz)]
+    line = [{"recv": at(d, 0, 0)} for d in range(1, nx)]
+    greet = zs + ys + [{"sweep": mate(k)} for k in (6, 4, 2)] + line
+
+    def tell(sem, device):
+        pl.semaphore_signal(sem, inc=1, device_id=device, device_id_type=MESH)
+
+    @pl.when(core == 1)
+    def _():
+        tell(barrier, {"sweep": sib})
+
     part = samples // PARTS
     mine = pl.ds(pl.multiple_of(core * half, half), half)
     theirs = pl.ds(pl.multiple_of((1 - core) * half, half), half)
@@ -73,19 +86,6 @@
     for c in loads[2:]:
         c.start()
 
-    barrier = pltpu.get_barrier_semaphore()
-    ys = [{"recv": at(0, d, 0)} for d in range(1, ny)]
-    zs = [{"recv": at(0, 0, d)} for d in range(1, nz)]
-    greet = [{"sweep": mate(k)} for k in range(2, ns, 2)]
-    greet += ys + zs + [{"recv": at(d, 0, 0)} for d in range(1, nx)]
-
-    def tell(sem, device):
-        pl.semaphore_signal(sem, inc=1, device_id=device, device_id_type=MESH)
-
-    @pl.when(core == 1)
-    def _():
-        tell(barrier, {"sweep": sib})
-
     @pl.when(core == 0)
     def _():
         pl.semaphore_wait(barrier, 1)
@@ -94,6 +94,8 @@
     @pl.when(core == 1)
     def _():
         pl.semaphore_wait(pair.at[0], 1)
+        for d in greet:
+            tell(barrier, d)
 
     trade = [
         pltpu.make_async_remote_copy(
@@ -105,11 +107,6 @@
     ]
     for c in trade:
         c.start()
-
-    @pl.when(core == 1)
-    def _():
-        for d in greet:
-            tell(barrier, d)
 
     l_pil.wait()
     l_cv.wait()
@@ -122,16 +119,33 @@
     onehot = (pick == col).astype(F32).astype(BF)
     cp = jnp.dot(onehot, pil[...], preferred_element_type=F32)
     cp = jnp.concatenate([cp, jnp.zeros((codes, samples - plen), F32)], axis=1)
-    for f in range(0, FINE, 2):
-        a = cp if f == 0 else pltpu.roll(cp, f, 1)
-        b = pltpu.roll(cp, f + 1, 1)
-        for g in range(SIDES):
-            both = jnp.concatenate([a[g * slots:(g + 1) * slots], b[g * slots:(g + 1) * slots]], axis=0)
-            wmat[g, f * slots:(f + 2) * slots, :] = both.astype(BF)
+
+    def build(g):
+        own_slots = cp[g * slots:(g + 1) * slots]
+        for f in range(0, FINE, 2):
+            both = [pltpu.roll(own_slots, v, 1) if v else own_slots for v in (f, f + 1)]
+            wmat[g, f * slots:(f + 2) * slots, :] = jnp.concatenate(both, axis=0).astype(BF)
+
+    build(1)
+
+    l_had.wait()
+
+    rect[samples:samples + LANES, :] = jnp.zeros((LANES, LANES), BF)
+    for i in range(PARTS):
+        own_rec[i].wait()
+        trade[i].wait_recv()
+        for b in range(i * part // LANES, (i + 1) * part // LANES):
+            blk = rec[:, :, :, b * LANES:(b + 1) * LANES].reshape(2 * held * half, LANES)
+            rect[b * LANES:(b + 1) * LANES, :] = blk.T
+
+    def copy1(k):
+        return pltpu.make_async_remote_copy(
+            src_ref=sb.at[k], dst_ref=rb.at[k - 1],
+            send_sem=s1_send.at[k - 1], recv_sem=s1_recv.at[k - 1],
+            device_id={"sweep": mate(k)}, device_id_type=MESH)
 
     lane = lax.broadcasted_iota(jnp.int32, (1, LANES), 1)
     group = lane // half
-    l_had.wait()
     norm = 1.0 / math.sqrt(codes)
     sweeps = [held * me + i for i in range(held)] + [held * sib + i for i in range(held)]
     coef = []
@@ -140,28 +154,6 @@
         for g, s in enumerate(sweeps):
             v = jnp.where(group == g, had[s, slot_code[q]].astype(F32) * norm, v)
         coef.append(v)
-    l_own.wait()
-    l_live.wait()
-    own_t = jnp.broadcast_to(own[...].astype(F32), (LANES, chans)).T
-    live_t = jnp.broadcast_to(live[...].astype(F32), (LANES, chans)).T
-    for c in range(owned):
-        v = cv[owned * me + c].astype(F32)
-        wgt[c * chans:(c + 1) * chans, :] = live_t * jnp.where(own_t == v, 1.25, 0.25)
-
-    rect[samples:samples + LANES, :] = jnp.zeros((LANES, LANES), BF)
-    for i in range(PARTS):
-        own_rec[i].wait()
-        trade[i].wait_recv()
-        for b in range(i * part // LANES, (i + 1) * part // LANES):
-            blk = rec[:, :, :, b * LANES:(b + 1) * LANES].reshape(2 * held * half, LANES)
-            rect[b * LANES:(b + 1) * LANES, :] = blk.T
-
-    def copy1(k):
-        return pltpu.make_async_remote_copy(
-            src_ref=sb.at[k], dst_ref=rb.at[k - 1],
-            send_sem=s1_send.at[k - 1], recv_sem=s1_recv.at[k - 1],
-            device_id={"sweep": mate(k)}, device_id_type=MESH)
-
     low = group < 2
     outer = (group == 0) | (group == 3)
     even = group % 2 == 0
@@ -187,6 +179,8 @@
     for g in (1, 0):
         for p in range(pairs):
             correlate(g, p)
+            if g == 1 and p == 0:
+                build(0)
             for k in range(g * ranks, (g + 1) * ranks):
                 decode(g, p, k)
         if g == 1:
@@ -205,8 +199,16 @@
             for d in ys:
                 tell(relay.at[0], d)
 
+    l_own.wait()
+    l_live.wait()
+    own_t = jnp.broadcast_to(own[...].astype(F32), (LANES, chans)).T
+    live_t = jnp.broadcast_to(live[...].astype(F32), (LANES, chans)).T
+    for c in range(owned):
+        v = cv[owned * me + c].astype(F32)
+        wgt[c * chans:(c + 1) * chans, :] = live_t * jnp.where(own_t == v, 1.25, 0.25)
+
     pl.semaphore_wait(relay.at[0], ny - 1)
-    for d in zs:
+    for d in line:
         tell(relay.at[1], d)
 
     first = jnp.full((FINE, LANES), core, jnp.int32) == 0
@@ -249,7 +251,7 @@
 
     steps = [(dx, dy, dz) for dx in range(nx) for dy in range(ny) for dz in range(nz)]
     steps.sort(key=lambda s: -(min(s[0], nx - s[0]) + min(s[1], ny - s[1]) + 4 * s[2]))
-    pl.semaphore_wait(relay.at[1], nz - 1)
+    pl.semaphore_wait(relay.at[1], nx - 1)
     for n, s in enumerate(steps[:-1]):
         j = at(*s)
         pltpu.make_async_remote_copy(

time: 31.7 us -> 31.2 us (0.984)
  Pallas kernels: 30.9 us -> 30.4 us
    pallas_call x1, Pallas kernels: 30.3 us -> 29.8 us  [local(): pl.pallas_call(functools.partial(kernel, ns, nr), out_shape=(vm((owned, c...]
where the time goes in v4:
time: 31.2 us; the launch traced here: 31 us
  Pallas kernels  30.4 us (97%)
  between operations  0.64 us (2%)
    pallas_call x1, Pallas kernels, local(): pl.pallas_call(functools.partial(kernel, ns, nr), out_shape=(vm((owned, c...  29.8 us
    pallas_call x1, Pallas kernels, local(): pl.pallas_call(deliver, out_shape=[jax.ShapeDtypeStruct(a.shape, a.dtype)...  0.65 us

profile of v4, /device:TPU:1, one launch (start us, length us, event | category | flops | bytes accessed | tf_op | source)
XLA Modules:
  0.0 31.0 jit_solution(12944346464415797046)
XLA Ops:
  0.6 29.8 %shard_map.95 = (f32[2,64,128]{2,1,0:T(8,128)S(1)}, f32[2,2,128]{2,1,0:T(2,128)S(1)}) custom-call(bf16[2,64,4096]{2,1,0:T(8,128)(2,1)} %rec_h.1, bf16[16,3968]{1,0:T(8,128)(2,1)} %pil_h.1, s32[16,16]{1,0:T(8,128)} %had_h.1, s32[16]{0:T(128)} %cv_h.1, s32[1,64]{1,0:T(1,128)} %bitcast.2, s32[1,64]{1,0:T(1,128)} %bitcast.3, bf16[2,128,128]{2,1,0:T(8,128)(2,1)} %fil_h.1, ...), custom_call_target="tpu_custom_call" | custom-call | tf_op jit(solution)/shard_map/pallas_call | solution.py:297
  30.4 0.7 %shard_map.96 = (f32[2,64,128]{2,1,0:T(8,128)}, f32[2,2,128]{2,1,0:T(2,128)}) custom-call(f32[2,64,128]{2,1,0:T(8,128)S(1)} %get-tuple-element.4.resp_v, f32[2,2,128]{2,1,0:T(2,128)S(1)} %get-tuple-element.5.grad_v), custom_call_target="tpu_custom_call" | custom-call | tf_op jit(solution)/shard_map/pallas_call | solution.py:320

commit v5 on v4

--- a/solution.py
+++ b/solution.py
@@ -51,7 +51,7 @@
         return ((x + dx) % nx * ny + (y + dy) % ny) * nz + (z + dz) % nz
 
     sib = mate(1)
-    order = [[6, 7, 4, 5], [2, 3, 1]]
+    order = [[7, 6, 5, 4], [3, 2, 1]]
     ranks = ns // SIDES
     slots = codes // SIDES
 
@@ -157,13 +157,11 @@
     low = group < 2
     outer = (group == 0) | (group == 3)
     even = group % 2 == 0
-    def correlate(g, p):
-        base = 2 * FINE * p
-        rhs = jnp.concatenate(
-            [rect[base:base + samples, :], rect[base + FINE:base + FINE + samples, :]], axis=1)
+    def correlate(g):
+        rhs = jnp.concatenate([rect[n * FINE:n * FINE + samples, :] for n in range(2 * pairs)], axis=1)
         acc = jnp.dot(wmat[g], rhs, preferred_element_type=F32)
-        xs[g, p, 0] = acc[:, :LANES]
-        xs[g, p, 1] = acc[:, LANES:]
+        for n in range(2 * pairs):
+            xs[g, n // 2, n % 2] = acc[:, n * LANES:(n + 1) * LANES]
 
     def decode(g, p, k):
         q = owned * (k % ranks)
@@ -177,10 +175,10 @@
         sb[k, p] = t.astype(BF)
 
     for g in (1, 0):
+        correlate(g)
+        if g == 1:
+            build(0)
         for p in range(pairs):
-            correlate(g, p)
-            if g == 1 and p == 0:
-                build(0)
             for k in range(g * ranks, (g + 1) * ranks):
                 decode(g, p, k)
         if g == 1:
@@ -213,24 +211,25 @@
 
     first = jnp.full((FINE, LANES), core, jnp.int32) == 0
     pieces = []
-    for ks in order:
-        for k in ks:
-            copy1(k).wait_recv()
+    l_fil.wait()
+    l_tgt.wait()
+    for k in (1, 2, 3):
+        copy1(k).wait_recv()
+    sums = [(sb[0, p].astype(F32) + rb[1, p].astype(F32), rb[0, p].astype(F32) + rb[2, p].astype(F32))
+            for p in range(pairs)]
+    for k in order[0]:
+        copy1(k).wait_recv()
     for p in range(pairs):
-        here = sb[0, p].astype(F32)
-        for k in (6, 4, 2):
+        here, there = sums[p]
+        for k in (4, 6):
             here = here + rb[k - 1, p].astype(F32)
-        there = rb[6, p].astype(F32)
-        for k in (5, 3, 1):
-            there = there + rb[k - 1, p].astype(F32)
+            there = there + rb[k, p].astype(F32)
         h0 = jnp.where(first, here, there)
         h1 = jnp.where(first, there, here)
         pieces.append(jnp.where(low, h0, pltpu.roll(h1, 2 * half, 1)))
         pieces.append(jnp.where(low, pltpu.roll(h0, 2 * half, 1), h1))
     dec_t = jnp.concatenate(pieces, axis=0).astype(BF)
     dec = dec_t.T
-    l_fil.wait()
-    l_tgt.wait()
     res = []
     for c in range(owned):
         lhs = jnp.concatenate([dec[(h * owned + c) * half:(h * owned + c + 1) * half, :] for h in range(2)], axis=0)

time: 31.2 us -> 30.9 us (level)
    pallas_call x1, Pallas kernels: 29.8 us -> 29.4 us  [local(): pl.pallas_call(functools.partial(kernel, ns, nr), out_shape=(vm((owned, c...]
where the time goes in v5:
time: 30.9 us; the launch traced here: 30.7 us
  Pallas kernels  30.1 us (97%)
  between operations  0.64 us (2%)
    pallas_call x1, Pallas kernels, local(): pl.pallas_call(functools.partial(kernel, ns, nr), out_shape=(vm((owned, c...  29.4 us
    pallas_call x1, Pallas kernels, local(): pl.pallas_call(deliver, out_shape=[jax.ShapeDtypeStruct(a.shape, a.dtype)...  0.65 us

profile of v5, /device:TPU:1, one launch (start us, length us, event | category | flops | bytes accessed | tf_op | source)
XLA Modules:
  0.0 30.7 jit_solution(17584770024741589622)
XLA Ops:
  0.6 29.4 %shard_map.95 = (f32[2,64,128]{2,1,0:T(8,128)S(1)}, f32[2,2,128]{2,1,0:T(2,128)S(1)}) custom-call(bf16[2,64,4096]{2,1,0:T(8,128)(2,1)} %rec_h.1, bf16[16,3968]{1,0:T(8,128)(2,1)} %pil_h.1, s32[16,16]{1,0:T(8,128)} %had_h.1, s32[16]{0:T(128)} %cv_h.1, s32[1,64]{1,0:T(1,128)} %bitcast.2, s32[1,64]{1,0:T(1,128)} %bitcast.3, bf16[2,128,128]{2,1,0:T(8,128)(2,1)} %fil_h.1, ...), custom_call_target="tpu_custom_call" | custom-call | tf_op jit(solution)/shard_map/pallas_call | solution.py:296
  30.1 0.7 %shard_map.96 = (f32[2,64,128]{2,1,0:T(8,128)}, f32[2,2,128]{2,1,0:T(2,128)}) custom-call(f32[2,64,128]{2,1,0:T(8,128)S(1)} %get-tuple-element.4.resp_v, f32[2,2,128]{2,1,0:T(2,128)S(1)} %get-tuple-element.5.grad_v), custom_call_target="tpu_custom_call" | custom-call | tf_op jit(solution)/shard_map/pallas_call | solution.py:319

commit v6 on v5

--- a/solution.py
+++ b/solution.py
@@ -248,11 +248,13 @@
     ch[...] = jnp.stack(
         [gs[c, pl.ds(i, nr, stride=rows), :] for c in range(owned) for i in range(rows)], axis=1).astype(BF)
 
-    steps = [(dx, dy, dz) for dx in range(nx) for dy in range(ny) for dz in range(nz)]
-    steps.sort(key=lambda s: -(min(s[0], nx - s[0]) + min(s[1], ny - s[1]) + 4 * s[2]))
+    def outward(i, n):
+        return n // 2 + (i + 1) // 2 * (1 - 2 * (i % 2))
+
     pl.semaphore_wait(relay.at[1], nx - 1)
-    for n, s in enumerate(steps[:-1]):
-        j = at(*s)
+    @pl.loop(0, nr - 1)
+    def _(n):
+        j = at(outward(n % nx, nx), outward(n // nx % ny, ny), nz - 1 - n // (nx * ny))
         pltpu.make_async_remote_copy(
             src_ref=ch.at[j], dst_ref=gb.at[n], send_sem=s2_send.at[0], recv_sem=s2_recv.at[0],
             device_id={"recv": j}, device_id_type=MESH).start()

time: 30.9 us -> 30.9 us (level)
  no operation moved by 1% of the time
where the time goes in v6:
time: 30.9 us; the launch traced here: 30.7 us
  Pallas kernels  30.1 us (97%)
  between operations  0.64 us (2%)
    pallas_call x1, Pallas kernels, local(): pl.pallas_call(functools.partial(kernel, ns, nr), out_shape=(vm((owned, c...  29.4 us
    pallas_call x1, Pallas kernels, local(): pl.pallas_call(deliver, out_shape=[jax.ShapeDtypeStruct(a.shape, a.dtype)...  0.65 us

profile of v6, /device:TPU:1, one launch (start us, length us, event | category | flops | bytes accessed | tf_op | source)
XLA Modules:
  0.0 30.7 jit_solution(15709195483047237169)
XLA Ops:
  0.6 29.4 %shard_map.95 = (f32[2,64,128]{2,1,0:T(8,128)S(1)}, f32[2,2,128]{2,1,0:T(2,128)S(1)}) custom-call(bf16[2,64,4096]{2,1,0:T(8,128)(2,1)} %rec_h.1, bf16[16,3968]{1,0:T(8,128)(2,1)} %pil_h.1, s32[16,16]{1,0:T(8,128)} %had_h.1, s32[16]{0:T(128)} %cv_h.1, s32[1,64]{1,0:T(1,128)} %bitcast.2, s32[1,64]{1,0:T(1,128)} %bitcast.3, bf16[2,128,128]{2,1,0:T(8,128)(2,1)} %fil_h.1, ...), custom_call_target="tpu_custom_call" | custom-call | tf_op jit(solution)/shard_map/pallas_call | solution.py:298
  30.1 0.7 %shard_map.96 = (f32[2,64,128]{2,1,0:T(8,128)}, f32[2,2,128]{2,1,0:T(2,128)}) custom-call(f32[2,64,128]{2,1,0:T(8,128)S(1)} %get-tuple-element.4.resp_v, f32[2,2,128]{2,1,0:T(2,128)S(1)} %get-tuple-element.5.grad_v), custom_call_target="tpu_custom_call" | custom-call | tf_op jit(solution)/shard_map/pallas_call | solution.py:321
